TPU v7x, 128 devices: a whole 4x4x4 slice. The times are simulated.
128 devices in a mesh: tm: 8 (over z, y_hi), feat: 16 (over y_lo, x, core).
Axes of the slice: x: 4, y: 4 (y_hi: 2, y_lo: 2; y = y_hi * 2 + y_lo), z: 4, core: 2. Of those that a mesh axis runs over, the one named last changes fastest.
Arguments:
- trajectory: float32 [32768, 2048], P('tm', 'feat'), may hold values from -8 to 9
Outputs:
- moments: float32 [4, 2048, 2048], P(None, 'feat', 'tm')
All inputs are finite; a program needn't handle non-finite values.
Results may differ from a plain program's by a relative error of at most 0.00035.
Values may be sent and summed in bfloat16 or wider, within the bound.
A program may use at most 128 MiB of HBM per device.

v0:
```python
import jax
import jax.numpy as jnp
from jax import lax
from jax.sharding import Mesh
from jax.sharding import PartitionSpec as P

HALO = 16
TM = ("tm_0", "tm_1")
lag_values = (0, 1, 4, 16)


def copy_for_each(array, axis):
    length = lax.axis_size(axis)
    return lax.all_to_all(
        jnp.broadcast_to(array[None], (length, *array.shape)), axis, 0, 0, tiled=True
    )


def over_copies(array, axis):
    return copy_for_each(array, axis).sum(axis=0)


def passed_along(value, axis, steps):
    count = lax.axis_size(axis)
    initial, last = (max(0, -steps), min(count, count - steps))
    return lax.ppermute(value, axis, [(source, source + steps) for source in range(initial, last)])


def summed_rows(array, axes, dim):
    for axis in axes:
        array = lax.psum_scatter(array, axis, scatter_dimension=dim, tiled=True)
    return array


def shards(trajectory):
    rows = trajectory.shape[0]
    frames = rows * lax.axis_size(TM)
    total = over_copies(jnp.sum(trajectory, axis=0), TM)
    mean = total / frames
    centered = (trajectory - mean).astype(jnp.bfloat16)
    gathered = lax.all_gather(centered, "feat", axis=1, tiled=True)
    tail = passed_along(gathered[:HALO], TM, -1)
    extended = jnp.concatenate([gathered, tail], axis=0)
    blocks = [
        lax.dot_general(
            centered,
            extended[lag : lag + rows],
            (((0,), (0,)), ((), ())),
            preferred_element_type=jnp.float32,
        )
        for lag in lag_values
    ]
    partial_sum = jnp.stack(blocks)
    summed = summed_rows(partial_sum, TM, 2)
    scales = jnp.sqrt(jnp.float32(frames) - jnp.array(lag_values, jnp.float32))
    return summed / scales[:, None, None]


def solution(mesh):
    torus = Mesh(mesh.devices.reshape(4, 2, mesh.shape["feat"]), ("tm_0", "tm_1", "feat"))
    in_specs = (P(TM, "feat"),)
    out_specs = P(None, "feat", TM)
    return jax.shard_map(
        shards, mesh=torus, in_specs=in_specs, out_specs=out_specs, check_vma=False
    )
```

profile of v0, /device:TPU:1, one launch (start us, length us, event | category | flops | bytes accessed | tf_op | source)
XLA Modules:
  0.0 244.3 jit_solution(2764542623991633967)
XLA Ops:
  6.5 0.0 all-gather.2.cloned.1.call-start
  6.5 2.1 reduce_sum.18
  8.7 14.8 %all_to_all.6 = f32[8,1,128]{2,1,0:T(1,128)S(1)} all-to-all(f32[8,1,128]{2,1,0:T(1,128)S(1)} %broadcast_in_dim.2), channel_id=1, replica_groups=mesh['tm_0'=4,'tm_1'=2,'feat'=16] {'tm_0','tm_1'}, dimensions={0} | all-to-all | bytes 8192 | tf_op jit(solution)/shard_map/all_to_all | solution.py:14
  23.5 2.7 %subtract_convert_fusion = bf16[4096,128]{1,0:T(8,128)(2,1)} fusion(f32[4096,128]{1,0:T(8,128)} %param.2, f32[128]{0:T(128)S(1)} %broadcast_multiply_fusion.1), kind=kLoop, calls=%fused_computation.11 | loop fusion | flops 1048576 | bytes 3146240 | tf_op jit(solution)/shard_map/convert_element_type | solution.py:40
  26.2 0.0 all-gather.2.cloned.1.call-update
  26.2 0.0 reduce-scatter.3.cloned.1.call-start
  26.3 98.0 %all-gather.2.cloned.1.call-done = bf16[4096,2048]{1,0:T(8,128)(2,1)} async-done(((bf16[4096,128]{1,0:T(8,128)(2,1)}), bf16[4096,2048]{1,0:T(8,128)(2,1)}) %all-gather.2.cloned.1.call-update) | async-done | bytes 16777232 | tf_op jit(solution)/shard_map/all_gather | solution.py:41
  124.3 0.0 slice-start
  124.3 1.6 slice.16
  125.9 0.0 slice-start.1
  125.9 0.0 slice-start.2
  125.9 0.0 slice-start.3
  125.9 1.5 collective-permute-start
  127.4 9.4 %constant_dynamic-update-slice_fusion.1 = bf16[4112,2048]{1,0:T(8,128)(2,1)S(1)} fusion(bf16[4096,2048]{1,0:T(8,128)(2,1)} %all-gather.2.cloned.1.call-done), kind=kLoop, calls=%fused_computation.14 | loop fusion | bytes 33554432
  136.8 0.0 slice-done
  136.8 0.0 slice-done.1
  136.8 0.0 slice-done.2
  136.8 0.0 slice-done.3
  136.9 4.6 %convolution_bitcast_fusion = f32[1,128,2048]{2,1,0:T(8,128)} fusion(bf16[4096,128]{1,0:T(8,128)(2,1)} %subtract_convert_fusion, bf16[4096,2048]{1,0:T(8,128)(2,1)S(1)} %bitcast.15), kind=kOutput, calls=%fused_computation.9 | convolution fusion | flops 2147483648 | bytes 18874368 | tf_op jit(solution)/shard_map/dot_general | solution.py:45
  141.5 0.0 collective-permute-done
  141.5 0.0 copy-start
  141.5 3.7 %fusion.9 = f32[1,128,2048]{2,1,0:T(8,128)S(1)} fusion(bf16[4096,128]{1,0:T(8,128)(2,1)} %subtract_convert_fusion, bf16[4112,2048]{1,0:T(8,128)(2,1)S(1)} %constant_dynamic-update-slice_fusion), kind=kOutput, calls=%fused_computation.8 | convolution fusion | flops 2147483648 | bytes 18874368 | tf_op jit(solution)/shard_map/dot_general | solution.py:45
  145.2 0.0 copy-done
  145.2 6.1 %fusion.12 = f32[1,128,2048]{2,1,0:T(8,128)} fusion(bf16[4096,128]{1,0:T(8,128)(2,1)S(1)} %copy-done, bf16[4112,2048]{1,0:T(8,128)(2,1)S(1)} %constant_dynamic-update-slice_fusion), kind=kOutput, calls=%fused_computation.10 | convolution fusion | flops 2147483648 | bytes 18874368 | tf_op jit(solution)/shard_map/dot_general | solution.py:45
  151.3 0.0 copy-start.1
  151.3 0.0 copy-start.2
  151.3 6.1 %fusion.6 = f32[1,128,2048]{2,1,0:T(8,128)} fusion(bf16[4096,128]{1,0:T(8,128)(2,1)S(1)} %copy-done, bf16[4112,2048]{1,0:T(8,128)(2,1)S(1)} %constant_dynamic-update-slice_fusion), kind=kOutput, calls=%fused_computation.7 | convolution fusion | flops 2147483648 | bytes 18874368 | tf_op jit(solution)/shard_map/dot_general | solution.py:45
  157.4 0.0 copy-done.1
  157.4 3.9 %pad_maximum_fusion = f32[4,128,2048]{2,1,0:T(8,128)} fusion(f32[1,128,2048]{2,1,0:T(8,128)S(1)} %fusion.9, f32[1,128,2048]{2,1,0:T(8,128)} %fusion.12, f32[1,128,2048]{2,1,0:T(8,128)} %fusion.6, f32[1,128,2048]{2,1,0:T(8,128)S(1)} %copy-done.1), kind=kLoop, calls=%fused_computation.6 | loop fusion | flops 3145728 | bytes 8388608 | tf_op jit(solution)/shard_map/stack | solution.py:53
  161.3 0.0 reduce-scatter.3.cloned.1.call-update
  161.3 0.0 reduce-scatter.5.cloned.1.call-start
  161.3 48.1 %reduce-scatter.3.cloned.1.call-done = f32[4,128,512]{2,1,0:T(8,128)} async-done(((f32[4,128,2048]{2,1,0:T(8,128)}), f32[4,128,512]{2,1,0:T(8,128)}) %reduce-scatter.3.cloned.1.call-update) | async-done | bytes 1048592 | tf_op jit(solution)/shard_map/reduce_scatter | solution.py:31
  209.4 0.0 reduce-scatter.5.cloned.1.call-update
  209.5 26.4 %reduce-scatter.5.cloned.1.call-done = f32[4,128,256]{2,1,0:T(8,128)} async-done(((f32[4,128,512]{2,1,0:T(8,128)}), f32[4,128,256]{2,1,0:T(8,128)}) %reduce-scatter.5.cloned.1.call-update) | async-done | bytes 524304 | tf_op jit(solution)/shard_map/reduce_scatter | solution.py:31
  235.9 0.0 copy-done.2
  235.9 1.9 broadcast_multiply_fusion
  (5 shorter events, 0.0 us)
Async XLA Ops:
  6.5 117.7 %all-gather.2.cloned.1.call-start = ((), (), s32[]{:S(2)}) async-start(), calls=%async_computation.3 | async-start | bytes 17825792 | tf_op jit(solution)/shard_map/all_gather | solution.py:41
  26.2 183.2 %reduce-scatter.3.cloned.1.call-start = ((), (), s32[]{:S(2)}) async-start(), calls=%async_computation.4 | async-start | bytes 5242880 | tf_op jit(solution)/shard_map/reduce_scatter | solution.py:31
  124.3 12.6 %slice-start = ((s8[16777216]{0:T(1024)(128)(4,1)}), s8[4194304]{0:T(1024)(128)(4,1)S(1)}, s32[]{:S(2)}) async-start(s8[16777216]{0:T(1024)(128)(4,1)} %bitcast.14), calls=%async_computation.6 | async-start | bytes 8388608
  125.9 10.9 %slice-start.1 = ((s8[16777216]{0:T(1024)(128)(4,1)}), s8[4194304]{0:T(1024)(128)(4,1)S(1)}, s32[]{:S(2)}) async-start(s8[16777216]{0:T(1024)(128)(4,1)} %bitcast.14), calls=%async_computation.7 | async-start | bytes 8388608
  125.9 10.9 %slice-start.2 = ((s8[16777216]{0:T(1024)(128)(4,1)}), s8[4194304]{0:T(1024)(128)(4,1)S(1)}, s32[]{:S(2)}) async-start(s8[16777216]{0:T(1024)(128)(4,1)} %bitcast.14), calls=%async_computation.8 | async-start | bytes 8388608
  125.9 11.0 %slice-start.3 = ((s8[16777216]{0:T(1024)(128)(4,1)}), s8[4194304]{0:T(1024)(128)(4,1)S(1)}, s32[]{:S(2)}) async-start(s8[16777216]{0:T(1024)(128)(4,1)} %bitcast.14), calls=%async_computation.9 | async-start | bytes 8388608
  125.9 15.6 %collective-permute-start = (bf16[16,2048]{1,0:T(8,128)(2,1)}, bf16[16,2048]{1,0:T(8,128)(2,1)S(1)}, u32[]{:S(2)}, u32[]{:S(2)}) collective-permute-start(bf16[16,2048]{1,0:T(8,128)(2,1)} %slice.16), channel_id=1, source_target_pairs={{16,0},{32,16},{48,32},{64,48},{80,64},{96,80},{112,96},{17,1},{33... | collective-permute-start | bytes 196616 | tf_op jit(solution)/shard_map/ppermute | solution.py:26
  141.5 3.7 %copy-start = (bf16[4096,128]{1,0:T(8,128)(2,1)S(1)}, bf16[4096,128]{1,0:T(8,128)(2,1)}, u32[]{:S(2)}) copy-start(bf16[4096,128]{1,0:T(8,128)(2,1)} %subtract_convert_fusion) | copy-start | bytes 3145732
  151.3 6.1 %copy-start.1 = (f32[1,128,2048]{2,1,0:T(8,128)S(1)}, f32[1,128,2048]{2,1,0:T(8,128)}, u32[]{:S(2)}) copy-start(f32[1,128,2048]{2,1,0:T(8,128)} %convolution_bitcast_fusion) | copy-start | bytes 3145732
  151.3 84.5 %copy-start.2 = (f32[4]{0:T(128)S(1)}, f32[4]{0:T(128)}, u32[]{:S(2)}) copy-start(f32[4]{0:T(128)} %constant.13) | copy-start | bytes 52
  161.3 74.6 %reduce-scatter.5.cloned.1.call-start = ((), (), s32[]{:S(2)}) async-start(), calls=%async_computation.5 | async-start | bytes 1572864 | tf_op jit(solution)/shard_map/reduce_scatter | solution.py:31
Sparse Core Ops, SparseCore 0:
  26.3 97.8 all-gather.1
  161.4 47.9 reduce-scatter.2
  211.9 23.8 reduce-scatter.4
where the time goes:
time: 245 us; the launch traced here: 244 us
  waiting for transfers between devices  173 us (71%)
  matrix products  20.5 us (8%)
  blocking collectives  14.8 us (6%)
  between operations  13.2 us (5%)
  local copies, waits for them, and re-layouts  11 us (4%)
  other arithmetic  10.6 us (4%)
    all_gather x1, waiting for transfers between devices, shards(): gathered = lax.all_gather(centered, 'feat', axis=1, tiled=True)  98 us
    reduce_scatter x2, waiting for transfers between devices, summed_rows(): array = lax.psum_scatter(array, axis, scatter_dimension=dim, tiled=True)  74.5 us
    dot_general x4, matrix products, shards(): lax.dot_general(centered, extended[lag:lag + rows], (((0,), (0,)), ((), (...  20.5 us
    all_to_all x1, blocking collectives, copy_for_each(): lax.all_to_all(jnp.broadcast_to(array[None], (length, *array.shape)), axi...  14.8 us
    unnamed x15, local copies, waits for them, and re-layouts  9.39 us
  transfers between devices with their start and end apart: 4, of which 3 were waited for; matrix products, arithmetic and copies ran while one was open for 6% of the time, Pallas kernels for 0%

commit v1 on v0

--- a/solution.py
+++ b/solution.py
@@ -38,7 +38,9 @@
     total = over_copies(jnp.sum(trajectory, axis=0), TM)
     mean = total / frames
     centered = (trajectory - mean).astype(jnp.bfloat16)
-    gathered = lax.all_gather(centered, "feat", axis=1, tiled=True)
+    gathered = jnp.concatenate(
+        lax.all_to_all(jnp.stack([centered] * lax.axis_size("feat")), "feat", 0, 0), axis=1
+    )
     tail = passed_along(gathered[:HALO], TM, -1)
     extended = jnp.concatenate([gathered, tail], axis=0)
     blocks = [

time: 245 us -> 368 us (1.50)
  blocking collectives: 14.8 us -> 205 us
  waiting for transfers between devices: 173 us -> 74.8 us
  matrix products: 20.5 us -> 54.5 us
    all_to_all x0 -> x1, blocking collectives: none -> 190 us  [shards(): lax.all_to_all(jnp.stack([centered] * lax.axis_size('feat')), 'feat', 0, 0)]
    all_gather x1 -> x0, waiting for transfers between devices: 98 us -> none  [shards(): gathered = lax.all_gather(centered, 'feat', axis=1, tiled=True)]
    dot_general x4, matrix products: 20.5 us -> 54.5 us  [shards(): lax.dot_general(centered, extended[lag:lag + rows], (((0,), (0,)), ((), (...]
    unnamed x15 -> x6, local copies, waits for them, and re-layouts: 9.39 us -> 5.72 us
  transfers between devices with their start and end apart: 4 -> 3, of which waited for: 3 -> 3; matrix products, arithmetic and copies ran while one was open for 6% -> 3% of each run, Pallas kernels for 0% -> 0%
where the time goes in v1:
time: 368 us; the launch traced here: 367 us
  blocking collectives  205 us (56%)
  waiting for transfers between devices  74.8 us (20%)
  matrix products  54.5 us (15%)
  between operations  13.5 us (4%)
  other arithmetic  9.65 us (3%)
  local copies, waits for them, and re-layouts  8.37 us (2%)
    all_to_all x1, blocking collectives, shards(): lax.all_to_all(jnp.stack([centered] * lax.axis_size('feat')), 'feat', 0, 0)  190 us
    reduce_scatter x2, waiting for transfers between devices, summed_rows(): array = lax.psum_scatter(array, axis, scatter_dimension=dim, tiled=True)  71.7 us
    dot_general x4, matrix products, shards(): lax.dot_general(centered, extended[lag:lag + rows], (((0,), (0,)), ((), (...  54.5 us
    all_to_all x1, blocking collectives, copy_for_each(): lax.all_to_all(jnp.broadcast_to(array[None], (length, *array.shape)), axi...  14.8 us
  transfers between devices with their start and end apart: 3, of which 3 were waited for; matrix products, arithmetic and copies ran while one was open for 3% of the time, Pallas kernels for 0%

profile of v1, /device:TPU:1, one launch (start us, length us, event | category | flops | bytes accessed | tf_op | source)
XLA Modules:
  0.0 367.3 jit_solution(17904002842989935466)
XLA Ops:
  6.5 0.0 reduce-scatter.3.cloned.1.call-start
  6.5 2.1 reduce_sum.18
  8.7 14.8 %all_to_all.11 = f32[8,1,128]{2,1,0:T(1,128)S(1)} all-to-all(f32[8,1,128]{2,1,0:T(1,128)S(1)} %broadcast_in_dim.2), channel_id=1, replica_groups=mesh['tm_0'=4,'tm_1'=2,'feat'=16] {'tm_0','tm_1'}, dimensions={0} | all-to-all | bytes 8192 | tf_op jit(solution)/shard_map/all_to_all | solution.py:14
  23.5 1.7 subtract_convert_fusion
  25.2 0.5 copy.10
  25.8 2.0 stack.12
  27.7 190.4 %all_to_all.12 = bf16[16,4096,128]{1,2,0:T(8,128)(2,1)S(1)} all-to-all(bf16[16,4096,128]{1,2,0:T(8,128)(2,1)S(1)} %stack.12), channel_id=1, replica_groups=mesh['tm_0'=4,'tm_1'=2,'feat'=16] {'feat'}, dimensions={0} | all-to-all | bytes 33554432 | tf_op jit(solution)/shard_map/all_to_all | solution.py:42
  218.1 0.0 copy-start
  218.1 5.7 %copy-done = bf16[16,4096,128]{1,2,0:T(8,128)(2,1)} copy-done((bf16[16,4096,128]{1,2,0:T(8,128)(2,1)}, bf16[16,4096,128]{1,2,0:T(8,128)(2,1)S(1)}, u32[]{:S(2)}) %copy-start) | copy-done | bytes 16777240
  223.8 0.1 slice.20
  224.0 1.3 collective-permute-start
  225.3 11.5 %convolution_bitcast_fusion = f32[1,128,2048]{2,1,0:T(8,128)S(1)} fusion(bf16[4096,128]{1,0:T(8,128)(2,1)S(1)} %subtract_convert_fusion, bf16[4096,2048]{0,1:T(8,128)(2,1)} %bitcast.19), kind=kOutput, calls=%fused_computation.13 | convolution fusion | flops 2147483648 | bytes 18874368 | tf_op jit(solution)/shard_map/dot_general | solution.py:47
  236.7 0.0 copy-start.1
  236.8 3.0 collective-permute-done
  239.8 15.2 %fusion.14 = f32[1,128,2048]{2,1,0:T(8,128)S(1)} fusion(bf16[4096,128]{1,0:T(8,128)(2,1)S(1)} %subtract_convert_fusion, bf16[16,2048]{0,1:T(8,128)(2,1)} %collective-permute-done, bf16[4096,2048]{0,1:T(8,128)(2,1)} %bitcast.20), kind=kOutput, calls=%fused_computation.15 | convolution fusion | flops 2181038080 | bytes 18939904 | tf_op jit(solution)/shard_map/dot_general | solution.py:47
  255.0 0.0 copy-done.1
  255.1 13.7 %fusion.10 = f32[1,128,2048]{2,1,0:T(8,128)} fusion(bf16[4096,128]{1,0:T(8,128)(2,1)S(1)} %subtract_convert_fusion, bf16[16,2048]{0,1:T(8,128)(2,1)} %collective-permute-done, bf16[4096,2048]{0,1:T(8,128)(2,1)S(1)} %bitcast.21), kind=kOutput, calls=%fused_computation.12 | convolution fusion | flops 2181038080 | bytes 18939904 | tf_op jit(solution)/shard_map/dot_general | solution.py:47
  268.8 0.0 copy-start.2
  268.8 14.0 %fusion.11 = f32[1,128,2048]{2,1,0:T(8,128)} fusion(bf16[4096,128]{1,0:T(8,128)(2,1)S(1)} %subtract_convert_fusion, bf16[16,2048]{0,1:T(8,128)(2,1)} %collective-permute-done, bf16[4096,2048]{0,1:T(8,128)(2,1)S(1)} %bitcast.22), kind=kOutput, calls=%fused_computation.14 | convolution fusion | flops 2181038080 | bytes 18939904 | tf_op jit(solution)/shard_map/dot_general | solution.py:47
  282.8 3.8 %pad_maximum_fusion.2 = f32[4,128,2048]{2,1,0:T(8,128)} fusion(f32[1,128,2048]{2,1,0:T(8,128)} %fusion.10, f32[1,128,2048]{2,1,0:T(8,128)} %fusion.11, f32[1,128,2048]{2,1,0:T(8,128)S(1)} %fusion.14, f32[1,128,2048]{2,1,0:T(8,128)S(1)} %convolution_bitcast_fusion), kind=kLoop, calls=%fused_computation.11 | loop fusion | flops 3145728 | bytes 8388608 | tf_op jit(solution)/shard_map/stack | solution.py:55
  286.6 0.0 reduce-scatter.3.cloned.1.call-update
  286.7 0.0 reduce-scatter.5.cloned.1.call-start
  286.7 45.4 %reduce-scatter.3.cloned.1.call-done = f32[4,128,512]{2,1,0:T(8,128)} async-done(((f32[4,128,2048]{2,1,0:T(8,128)}), f32[4,128,512]{2,1,0:T(8,128)}) %reduce-scatter.3.cloned.1.call-update) | async-done | bytes 1048592 | tf_op jit(solution)/shard_map/reduce_scatter | solution.py:31
  332.1 0.0 reduce-scatter.5.cloned.1.call-update
  332.1 26.4 %reduce-scatter.5.cloned.1.call-done = f32[4,128,256]{2,1,0:T(8,128)} async-done(((f32[4,128,512]{2,1,0:T(8,128)}), f32[4,128,256]{2,1,0:T(8,128)}) %reduce-scatter.5.cloned.1.call-update) | async-done | bytes 524304 | tf_op jit(solution)/shard_map/reduce_scatter | solution.py:31
  358.5 0.0 copy-done.2
  358.5 1.9 broadcast_multiply_fusion
  (3 shorter events, 0.0 us)
Async XLA Ops:
  6.5 325.5 %reduce-scatter.3.cloned.1.call-start = ((), (), s32[]{:S(2)}) async-start(), calls=%async_computation.4 | async-start | bytes 5242880 | tf_op jit(solution)/shard_map/reduce_scatter | solution.py:31
  218.1 5.7 %copy-start = (bf16[16,4096,128]{1,2,0:T(8,128)(2,1)}, bf16[16,4096,128]{1,2,0:T(8,128)(2,1)S(1)}, u32[]{:S(2)}) copy-start(bf16[16,4096,128]{1,2,0:T(8,128)(2,1)S(1)} %all_to_all.12) | copy-start | bytes 50331652
  224.0 15.8 %collective-permute-start = (bf16[16,2048]{0,1:T(8,128)(2,1)S(1)}, bf16[16,2048]{0,1:T(8,128)(2,1)}, u32[]{:S(2)}, u32[]{:S(2)}) collective-permute-start(bf16[16,2048]{0,1:T(8,128)(2,1)S(1)} %bitcast.23), channel_id=1, source_target_pairs={{16,0},{32,16},{48,32},{64,48},{80,64},{96,80},{112,96},{17,1},{33... | collective-permute-start | bytes 196616 | tf_op jit(solution)/shard_map/ppermute | solution.py:26
  236.7 18.3 %copy-start.1 = (bf16[16,4096,128]{1,2,0:T(8,128)(2,1)S(1)}, bf16[16,4096,128]{1,2,0:T(8,128)(2,1)}, u32[]{:S(2)}) copy-start(bf16[16,4096,128]{1,2,0:T(8,128)(2,1)} %copy-done) | copy-start | bytes 50331652
  268.8 89.7 %copy-start.2 = (f32[4]{0:T(128)S(1)}, f32[4]{0:T(128)}, u32[]{:S(2)}) copy-start(f32[4]{0:T(128)} %constant.13) | copy-start | bytes 52
  286.7 71.8 %reduce-scatter.5.cloned.1.call-start = ((), (), s32[]{:S(2)}) async-start(), calls=%async_computation.5 | async-start | bytes 1572864 | tf_op jit(solution)/shard_map/reduce_scatter | solution.py:31
Sparse Core Ops, SparseCore 0:
  286.8 45.2 reduce-scatter.2
  334.5 23.8 reduce-scatter.4
